TPU v7x, 32 devices: a whole 2x2x4 slice. The times are simulated.
32 devices in a mesh: groups: 2 (over x), mom: 4 (over y, core), en: 4 (over z).
Axes of the slice: x: 2, y: 2, z: 4, core: 2. Of those that a mesh axis runs over, the one named last changes fastest.
Arguments:
- green_blocks: bfloat16 [16, 8, 2, 2, 256, 256], P(('groups', 'mom'), 'en'), parts along dimension 0, may hold values from -6 to 6
- hopping: bfloat16 [6, 256, 256], P('groups'), parts along dimension 0, may hold values from -0.375 to 0.375
- phonons: bfloat16 [16, 3, 2, 256, 256], P(('groups', 'en')), parts along dimension 0, may hold values from -1.796875 to 1.796875
- phonon_pick: int32 [4], replicated, may hold values from 0 to 7
- momentum_offsets: int32 [4, 8], P(None, 'mom'), may hold values from 0 to 1
- energy_map: int32 [4, 8], P(None, 'en'), may hold values from 0 to 1
Outputs:
- self_energy: float32 [16, 8, 2, 2, 256, 256], P(('groups', 'mom'), 'en'), parts along dimension 0
There are 2 independent parts, one for each index of `groups`. A program takes and returns all parts, laid end to end along the dimension named above; an argument that names none is the same for every part. Nothing has to cross between parts.
All inputs are finite; a program needn't handle non-finite values.
Results may differ from a plain program's by a relative error of at most 0.0029.
Values may be sent and summed in bfloat16 or wider, within the bound.
A program may use at most 128 MiB of HBM per device.

v0:
```python
import functools

import jax
import jax.numpy as jnp
from jax import lax
from jax.experimental import pallas as pl
from jax.experimental.pallas import tpu as pltpu
from jax.sharding import PartitionSpec as P

STEPS = 4
LAG = 2
MESH = pl.DeviceIdType.MESH


def kernel(
    n_mom, n_en, pick_ref, mom_ref, map_ref, green, hop, phon, out,
    near, low, top, right_in, left_in, weights,
    far_s, far_r, high_s, high_r, own_s, own_r, pass_s, pass_r,
    rt_s, rt_r, lt_s, lt_r, half_s, half_r,
):
    mom, z = lax.axis_index("mom"), lax.axis_index("en")
    core = lax.rem(mom, 2)
    sibling = mom + 1 - 2 * core
    up = lax.rem(mom + 2, n_mom)
    down = lax.rem(mom + n_mom - 2, n_mom)
    two = n_mom == 4
    slots, modes, _, rows, cols = phon.shape
    pieces = len(near)
    half = rows // 2
    mine = pl.ds(pl.multiple_of(core * half, half), half)
    chunks = STEPS * modes
    last = n_en - 1

    barrier = pltpu.get_barrier_semaphore()
    for other in (sibling, up) if two else (sibling, up, down):
        pl.semaphore_signal(barrier, inc=1, device_id={"mom": other}, device_id_type=MESH)

    @pl.when(z > 0)
    def _():
        pl.semaphore_signal(barrier, inc=1, device_id={"en": z - 1}, device_id_type=MESH)

    @pl.when(z < last)
    def _():
        pl.semaphore_signal(barrier, inc=1, device_id={"en": z + 1}, device_id_type=MESH)

    out[...] = jnp.zeros_like(out)
    greeted = (2 if two else 3) + (z > 0).astype(jnp.int32) + (z < last).astype(jnp.int32)
    pl.semaphore_wait(barrier, greeted)

    def remote(src, dst, send, recv, **device):
        return pltpu.make_async_remote_copy(
            src_ref=src, dst_ref=dst, send_sem=send, recv_sem=recv, device_id=device, device_id_type=MESH
        )

    def part(i):
        return green.at[:, :, i // 2, i % 2]

    def far(i):
        return remote(part(i), low[i], far_s.at[i], far_r.at[i], mom=up)

    def high(i):
        return remote(part(i), top[i], high_s.at[i], high_r.at[i], mom=down)

    def own(i):
        return remote(part(i), near[i].at[core], own_s.at[i], own_r.at[i], mom=sibling)

    def passed(i, source):
        return remote((low if source == 2 else top)[i], near[i].at[1 - core], pass_s.at[i], pass_r.at[i], mom=sibling)

    def rightward(q):
        return remote(right_in.at[q], right_in.at[q], rt_s.at[q], rt_r.at[q], en=z + 1)

    def leftward(q):
        return remote(left_in.at[q], left_in.at[q], lt_s.at[q], lt_r.at[q], en=z - 1)

    def share(q):
        return remote(weights.at[q, :, mine], weights.at[q, :, mine], half_s.at[q], half_r.at[q], mom=sibling)

    for i in range(pieces):
        far(i).start()
        if not two:
            high(i).start()
    for i in range(pieces):
        own(i).start()

    def forward(i):
        far(i).wait_recv()
        if two:
            passed(i, 2).start()
        else:
            high(i).wait_recv()

            @pl.when(core == 0)
            def _():
                passed(i, 3).start()

            @pl.when(core == 1)
            def _():
                passed(i, 2).start()

    def mix(q, buffer, at_end, arrival):
        point = pick_ref[q // modes]
        local = phon[lax.rem(point, slots), lax.rem(q, modes), :, mine]

        @pl.when(at_end)
        def _():
            buffer[q] = local

        @pl.when(jnp.logical_not(at_end))
        def _():
            arrival(q).wait_recv()
            buffer[q] = jnp.where(lax.div(point, slots) == z, local, buffer[q])

    def tick(t):
        q_right = t - LAG * z
        q_left = t - LAG * (last - z)
        q_done = t - LAG * jnp.maximum(z, last - z)

        @pl.when((q_right >= 0) & (q_right < chunks))
        def _():
            mix(q_right, right_in, z == 0, rightward)

            @pl.when(z < last)
            def _():
                rightward(q_right).start()

        @pl.when((q_left >= 0) & (q_left < chunks))
        def _():
            mix(q_left, left_in, z == last, leftward)

            @pl.when(z > 0)
            def _():
                leftward(q_left).start()

        @pl.when((q_done >= 0) & (q_done < chunks))
        def _():
            owner = lax.div(pick_ref[q_done // modes], slots)
            weights[q_done, :, mine] = jnp.where(owner <= z, right_in[q_done], left_in[q_done])
            share(q_done).start()

    def unit(step, i):
        source = 2 if two and step == 3 else step
        cell, imag = i // 2, i % 2

        def pair(j, carry):
            k, e = j // 2, j % 2
            m, n = mom_ref[step, k], map_ref[step, e]
            block = near[i][step, m, n] if step < 2 else (low if source == 2 else top)[i][m, n]
            real_sum = out[k, e, cell, 0]
            imag_sum = out[k, e, cell, 1]
            for a in range(modes):
                left = jnp.dot(hop[a], block, preferred_element_type=jnp.float32).astype(jnp.bfloat16)
                right = jnp.dot(left, hop[a], preferred_element_type=jnp.float32)
                w_re = weights[step * modes + a, 0].astype(jnp.float32)
                w_im = weights[step * modes + a, 1].astype(jnp.float32)
                if imag:
                    real_sum = real_sum - right * w_im
                    imag_sum = imag_sum + right * w_re
                else:
                    real_sum = real_sum + right * w_re
                    imag_sum = imag_sum + right * w_im
            out[k, e, cell, 0] = real_sum
            out[k, e, cell, 1] = imag_sum
            return carry

        lax.fori_loop(0, 4, pair, 0)

    seen = set()

    def need(step, i):
        if ("w", step) not in seen:
            seen.add(("w", step))
            for a in range(modes):
                share(step * modes + a).wait_recv()
        if step < 2 and ("g", i) not in seen:
            seen.add(("g", i))
            own(i).wait_recv()
            passed(i, 2).wait_recv()

    base = LAG * last + modes
    forwards = {base - 4: 0, base: 1, base + 4: 2, base + 8: 3}
    order = [
        (0, 0), (0, 1), (1, 0), (1, 1), None, (2, 0), (2, 1), (0, 2), (1, 2), (2, 2),
        (3, 0), (3, 1), (3, 2), (2, 3), (3, 3), (0, 3), (1, 3),
    ]
    sent = 0
    total = chunks + LAG * last
    for t in range(max(total, base + len(order))):
        if t < total:
            tick(t)
        if t in forwards:
            forward(forwards[t])
        if 0 <= t - base < len(order) and order[t - base]:
            step, i = order[t - base]
            need(step, i)
            unit(step, i)

    for i in range(pieces):
        far(i).wait_send()
        own(i).wait_send()
        passed(i, 2).wait_send()
        if not two:
            high(i).wait_send()

    def settle(q, carry):
        @pl.when(z < last)
        def _():
            rightward(q).wait_send()

        @pl.when(z > 0)
        def _():
            leftward(q).wait_send()

        share(q).wait_send()
        return carry

    lax.fori_loop(0, chunks, settle, 0)


def on_device(green_blocks, hopping, phonons, phonon_pick, momentum_offsets, energy_map):
    modes = hopping.shape[0]
    rows, cols = hopping.shape[1:]
    k_dev, e_dev, cells, parts = green_blocks.shape[:4]
    pieces = cells * parts
    chunks = STEPS * modes
    two = lax.axis_size("mom") == 4
    dma = pltpu.SemaphoreType.DMA
    vmem = pl.BlockSpec(memory_space=pltpu.VMEM)
    smem = pl.BlockSpec(memory_space=pltpu.SMEM)
    return pl.pallas_call(
        functools.partial(kernel, lax.axis_size("mom"), lax.axis_size("en")),
        out_shape=jax.ShapeDtypeStruct(green_blocks.shape, jnp.float32),
        in_specs=[smem, smem, smem, pl.BlockSpec(memory_space=pl.ANY), vmem, vmem],
        out_specs=vmem,
        scratch_shapes=[
            [pltpu.VMEM((2, k_dev, e_dev, rows, cols), jnp.bfloat16)] * pieces,
            [pltpu.VMEM((k_dev, e_dev, rows, cols), jnp.bfloat16)] * pieces,
            [pltpu.VMEM((k_dev, e_dev, rows, cols), jnp.bfloat16)] * (0 if two else pieces),
            pltpu.VMEM((chunks, 2, rows // 2, cols), jnp.bfloat16),
            pltpu.VMEM((chunks, 2, rows // 2, cols), jnp.bfloat16),
            pltpu.VMEM((chunks, 2, rows, cols), jnp.bfloat16),
        ]
        + [dma((pieces,))] * 8
        + [dma((chunks,))] * 6,
        compiler_params=pltpu.CompilerParams(
            collective_id=0, has_side_effects=True, vmem_limit_bytes=48 * 2**20
        ),
        cost_estimate=pl.CostEstimate(flops=13 * 10**9, bytes_accessed=8 * 2**20, transcendentals=0),
    )(phonon_pick, momentum_offsets, energy_map, green_blocks, hopping, phonons)


def solution(mesh):
    placed = (
        P(("groups", "mom"), "en", None, None, None, None),
        P("groups", None, None),
        P(("groups", "en"), None, None, None, None),
        P(),
        P(None, "mom"),
        P(None, "en"),
    )
    return jax.shard_map(
        on_device,
        mesh=mesh,
        in_specs=placed,
        out_specs=P(("groups", "mom"), "en", None, None, None, None),
        check_vma=False,
    )
```

profile of v0, /device:TPU:0, one launch (start us, length us, event | category | flops | bytes accessed | tf_op | source)
XLA Modules:
  0.0 84.3 jit_solution(16905976201732933956)
XLA Ops:
  0.0 0.8 copy.7.mom_ref
  0.8 0.8 copy.8.map_ref
  1.5 0.0 copy-start
  1.5 1.6 %copy-done = bf16[2,2,2,2,256,256]{5,4,3,2,1,0:T(8,128)(2,1)S(1)} copy-done((bf16[2,2,2,2,256,256]{5,4,3,2,1,0:T(8,128)(2,1)S(1)}, bf16[2,2,2,2,256,256]{5,4,3,2,1,0:T(8,128)(2,1)}, u32[]{:S(2)}) %copy-start) | copy-done | bytes 2097176
  3.1 0.0 copy-start.1
  3.1 1.4 %copy-done.1 = bf16[2,3,2,256,256]{4,3,2,1,0:T(8,128)(2,1)S(1)} copy-done((bf16[2,3,2,256,256]{4,3,2,1,0:T(8,128)(2,1)S(1)}, bf16[2,3,2,256,256]{4,3,2,1,0:T(8,128)(2,1)}, u32[]{:S(2)}) %copy-start.1) | copy-done | bytes 1572888
  4.5 0.0 copy-start.2
  4.5 1.0 %copy-done.2 = bf16[3,256,256]{2,1,0:T(8,128)(2,1)S(1)} copy-done((bf16[3,256,256]{2,1,0:T(8,128)(2,1)S(1)}, bf16[3,256,256]{2,1,0:T(8,128)(2,1)}, u32[]{:S(2)}) %copy-start.2) | copy-done | bytes 393240
  5.5 0.0 copy-start.3
  5.5 0.7 copy-done.3
  6.2 73.5 %shard_map.64 = f32[2,2,2,2,256,256]{5,4,3,2,1,0:T(8,128)} custom-call(s32[4]{0:T(128)S(1)} %copy-done.3, s32[4,2]{1,0:T(4,128)S(1)} %copy.7.mom_ref, s32[4,2]{1,0:T(4,128)S(1)} %copy.8.map_ref, bf16[2,2,2,2,256,256]{5,4,3,2,1,0:T(8,128)(2,1)S(1)} %copy-done, bf16[3,256,256]{2,1,0:T(8,128)(2,1)S(1)} %copy-done.2, bf16[2,3,2,256,256]{4,3,2,1,0:T(8,128)(2,1)S(1)} %copy-done.1), custom_call_target="tpu_custom_call" | custom-call | flops 12999999488 | bytes 8388608 | tf_op jit(solution)/shard_map/pallas_call | solution.py:230
  79.7 4.6 %copy.10 = f32[2,2,2,2,256,256]{5,4,3,2,1,0:T(8,128)} copy(f32[2,2,2,2,256,256]{5,4,3,2,1,0:T(8,128)} %shard_map.64) | data formatting | bytes 8388608
Async XLA Ops:
  1.5 1.6 %copy-start = (bf16[2,2,2,2,256,256]{5,4,3,2,1,0:T(8,128)(2,1)S(1)}, bf16[2,2,2,2,256,256]{5,4,3,2,1,0:T(8,128)(2,1)}, u32[]{:S(2)}) copy-start(bf16[2,2,2,2,256,256]{5,4,3,2,1,0:T(8,128)(2,1)} %green.1) | copy-start | bytes 6291460
  3.1 1.4 %copy-start.1 = (bf16[2,3,2,256,256]{4,3,2,1,0:T(8,128)(2,1)S(1)}, bf16[2,3,2,256,256]{4,3,2,1,0:T(8,128)(2,1)}, u32[]{:S(2)}) copy-start(bf16[2,3,2,256,256]{4,3,2,1,0:T(8,128)(2,1)} %phon.1) | copy-start | bytes 4718596
  4.5 1.0 %copy-start.2 = (bf16[3,256,256]{2,1,0:T(8,128)(2,1)S(1)}, bf16[3,256,256]{2,1,0:T(8,128)(2,1)}, u32[]{:S(2)}) copy-start(bf16[3,256,256]{2,1,0:T(8,128)(2,1)} %hop.1) | copy-start | bytes 1179652
  5.5 0.7 copy-start.3
where the time goes:
time: 84.6 us; the launch traced here: 84.3 us
  Pallas kernels  73.5 us (87%)
  local copies, waits for them, and re-layouts  10.8 us (13%)
    pallas_call x1, Pallas kernels, on_device(): pl.pallas_call(functools.partial(kernel, lax.axis_size('mom'), lax.axis_s...  73.5 us
    unnamed x11, local copies, waits for them, and re-layouts  10.8 us

commit v1 on v0

--- a/solution.py
+++ b/solution.py
@@ -9,12 +9,14 @@
 
 STEPS = 4
 LAG = 2
+STRIP = 16
 MESH = pl.DeviceIdType.MESH
 
 
 def kernel(
-    n_mom, n_en, pick_ref, mom_ref, map_ref, green, hop, phon, out,
-    near, low, top, right_in, left_in, weights,
+    n_mom, n_en, pick_in, mom_in, map_in, green, hop_in, phon_in, out,
+    pick_ref, mom_ref, map_ref, hop, phon, near, low, top, low_t, top_t, own_t, near_t,
+    right_in, left_in, weights, load,
     far_s, far_r, high_s, high_r, own_s, own_r, pass_s, pass_r,
     rt_s, rt_r, lt_s, lt_r, half_s, half_r,
 ):
@@ -24,13 +26,22 @@
     up = lax.rem(mom + 2, n_mom)
     down = lax.rem(mom + n_mom - 2, n_mom)
     two = n_mom == 4
-    slots, modes, _, rows, cols = phon.shape
+    slots, modes, _, rows, cols = phon_in.shape
     pieces = len(near)
     half = rows // 2
     mine = pl.ds(pl.multiple_of(core * half, half), half)
     chunks = STEPS * modes
     last = n_en - 1
 
+    loads = [
+        pltpu.make_async_copy(src, dst, load.at[i])
+        for i, (src, dst) in enumerate(
+            ((pick_in, pick_ref), (phon_in.at[:, :, :, mine], phon), (mom_in, mom_ref), (map_in, map_ref), (hop_in, hop))
+        )
+    ]
+    for copy in loads:
+        copy.start()
+
     barrier = pltpu.get_barrier_semaphore()
     for other in (sibling, up) if two else (sibling, up, down):
         pl.semaphore_signal(barrier, inc=1, device_id={"mom": other}, device_id_type=MESH)
@@ -62,10 +73,10 @@
         return remote(part(i), top[i], high_s.at[i], high_r.at[i], mom=down)
 
     def own(i):
-        return remote(part(i), near[i].at[core], own_s.at[i], own_r.at[i], mom=sibling)
+        return remote(part(i), near[i].at[0], own_s.at[i], own_r.at[i], mom=sibling)
 
     def passed(i, source):
-        return remote((low if source == 2 else top)[i], near[i].at[1 - core], pass_s.at[i], pass_r.at[i], mom=sibling)
+        return remote((low if source == 2 else top)[i], near[i].at[1], pass_s.at[i], pass_r.at[i], mom=sibling)
 
     def rightward(q):
         return remote(right_in.at[q], right_in.at[q], rt_s.at[q], rt_r.at[q], en=z + 1)
@@ -82,6 +93,8 @@
             high(i).start()
     for i in range(pieces):
         own(i).start()
+    loads[0].wait()
+    loads[1].wait()
 
     def forward(i):
         far(i).wait_recv()
@@ -100,7 +113,7 @@
 
     def mix(q, buffer, at_end, arrival):
         point = pick_ref[q // modes]
-        local = phon[lax.rem(point, slots), lax.rem(q, modes), :, mine]
+        local = phon[lax.rem(point, slots), lax.rem(q, modes)]
 
         @pl.when(at_end)
         def _():
@@ -138,62 +151,98 @@
             weights[q_done, :, mine] = jnp.where(owner <= z, right_in[q_done], left_in[q_done])
             share(q_done).start()
 
-    def unit(step, i):
-        source = 2 if two and step == 3 else step
+    def transform(source, turned):
+        def block(m, carry):
+            left = [
+                jnp.dot(hop[...], source[m, n], preferred_element_type=jnp.float32).astype(jnp.bfloat16)
+                for n in range(2)
+            ]
+            for a in range(modes):
+                span = slice(a * rows, (a + 1) * rows)
+                for n in range(2):
+                    turned[a, m, n] = jnp.dot(left[n][span], hop[span], preferred_element_type=jnp.float32)
+            return carry
+
+        lax.fori_loop(0, 2, block, 0)
+
+    def weigh(turned, step, i):
         cell, imag = i // 2, i % 2
 
-        def pair(j, carry):
-            k, e = j // 2, j % 2
-            m, n = mom_ref[step, k], map_ref[step, e]
-            block = near[i][step, m, n] if step < 2 else (low if source == 2 else top)[i][m, n]
-            real_sum = out[k, e, cell, 0]
-            imag_sum = out[k, e, cell, 1]
-            for a in range(modes):
-                left = jnp.dot(hop[a], block, preferred_element_type=jnp.float32).astype(jnp.bfloat16)
-                right = jnp.dot(left, hop[a], preferred_element_type=jnp.float32)
-                w_re = weights[step * modes + a, 0].astype(jnp.float32)
-                w_im = weights[step * modes + a, 1].astype(jnp.float32)
-                if imag:
-                    real_sum = real_sum - right * w_im
-                    imag_sum = imag_sum + right * w_re
-                else:
-                    real_sum = real_sum + right * w_re
-                    imag_sum = imag_sum + right * w_im
-            out[k, e, cell, 0] = real_sum
-            out[k, e, cell, 1] = imag_sum
+        def strip(r, carry):
+            span = pl.ds(pl.multiple_of(r * STRIP, STRIP), STRIP)
+            w = [[weights[step * modes + a, p, span].astype(jnp.float32) for p in range(2)] for a in range(modes)]
+            for k in range(2):
+                for e in range(2):
+                    m, n = mom_ref[k, step], map_ref[e, step]
+                    t = [turned[a, m, n, span] for a in range(modes)]
+                    with_re = sum(t[a] * w[a][0] for a in range(modes))
+                    with_im = sum(t[a] * w[a][1] for a in range(modes))
+                    if imag:
+                        out[k, e, cell, 0, span] -= with_im
+                        out[k, e, cell, 1, span] += with_re
+                    else:
+                        out[k, e, cell, 0, span] += with_re
+                        out[k, e, cell, 1, span] += with_im
             return carry
 
-        lax.fori_loop(0, 4, pair, 0)
-
-    seen = set()
-
-    def need(step, i):
-        if ("w", step) not in seen:
-            seen.add(("w", step))
-            for a in range(modes):
-                share(step * modes + a).wait_recv()
-        if step < 2 and ("g", i) not in seen:
-            seen.add(("g", i))
-            own(i).wait_recv()
-            passed(i, 2).wait_recv()
+        lax.fori_loop(0, rows // STRIP, strip, 0)
+
+    def far_turn(i):
+        transform(low[i], low_t[i])
+        if not two:
+            transform(top[i], top_t[i])
+
+    def third(i):
+        weigh(low_t[i], 2, i)
+
+    def fourth(i):
+        weigh(low_t[i] if two else top_t[i], 3, i)
+
+    def own_turn(i):
+        own(i).wait_recv()
+        transform(near[i].at[0], own_t[i] if two else near_t)
+
+    def own_weigh(i):
+        if not two:
+            own_turn(i)
+        weigh(own_t[i] if two else near_t, 1 - core, i)
+
+    def sibling_far(i):
+        passed(i, 2).wait_recv()
+        transform(near[i].at[1], near_t)
+        weigh(near_t, core, i)
+
+    def arrived(step):
+        for a in range(modes):
+            share(step * modes + a).wait_recv()
 
     base = LAG * last + modes
-    forwards = {base - 4: 0, base: 1, base + 4: 2, base + 8: 3}
-    order = [
-        (0, 0), (0, 1), (1, 0), (1, 1), None, (2, 0), (2, 1), (0, 2), (1, 2), (2, 2),
-        (3, 0), (3, 1), (3, 2), (2, 3), (3, 3), (0, 3), (1, 3),
-    ]
-    sent = 0
     total = chunks + LAG * last
-    for t in range(max(total, base + len(order))):
+    plan = {
+        base - 3: [(forward, 0)],
+        base - 2: [(far_turn, 0)],
+        base: [(arrived, 0)],
+        base + 2: [(forward, 1), (far_turn, 1)],
+        base + 3: [(arrived, 1), (own_weigh, 0), (own_weigh, 1), (sibling_far, 0)],
+        base + 4: [(own_weigh, 2), (own_weigh, 3)],
+        base + 5: [(sibling_far, 1)],
+        base + 6: [(arrived, 2), (forward, 2), (third, 0)],
+        base + 7: [(far_turn, 2), (third, 1)],
+        base + 8: [(third, 2)],
+        base + 9: [
+            (sibling_far, 2), (arrived, 3), (fourth, 0), (fourth, 1), (fourth, 2),
+            (forward, 3), (far_turn, 3), (third, 3), (fourth, 3), (sibling_far, 3),
+        ],
+    }
+    if two:
+        plan.update({1 + i: [(own_turn, i)] for i in range(pieces)})
+    for copy in loads[2:]:
+        copy.wait()
+    for t in range(max(total, base + 10)):
         if t < total:
             tick(t)
-        if t in forwards:
-            forward(forwards[t])
-        if 0 <= t - base < len(order) and order[t - base]:
-            step, i = order[t - base]
-            need(step, i)
-            unit(step, i)
+        for task, which in plan.get(t, []):
+            task(which)
 
     for i in range(pieces):
         far(i).wait_send()
@@ -226,27 +275,40 @@
     two = lax.axis_size("mom") == 4
     dma = pltpu.SemaphoreType.DMA
     vmem = pl.BlockSpec(memory_space=pltpu.VMEM)
-    smem = pl.BlockSpec(memory_space=pltpu.SMEM)
+    hbm = pl.BlockSpec(memory_space=pl.ANY)
+    turned = pltpu.VMEM((modes, k_dev, e_dev, rows, cols), jnp.float32)
     return pl.pallas_call(
         functools.partial(kernel, lax.axis_size("mom"), lax.axis_size("en")),
         out_shape=jax.ShapeDtypeStruct(green_blocks.shape, jnp.float32),
-        in_specs=[smem, smem, smem, pl.BlockSpec(memory_space=pl.ANY), vmem, vmem],
+        in_specs=[hbm] * 6,
         out_specs=vmem,
         scratch_shapes=[
+            pltpu.SMEM(phonon_pick.shape, jnp.int32),
+            pltpu.SMEM(momentum_offsets.shape[::-1], jnp.int32),
+            pltpu.SMEM(energy_map.shape[::-1], jnp.int32),
+            pltpu.VMEM((modes * rows, cols), jnp.bfloat16),
+            pltpu.VMEM((*phonons.shape[:3], rows // 2, cols), jnp.bfloat16),
             [pltpu.VMEM((2, k_dev, e_dev, rows, cols), jnp.bfloat16)] * pieces,
             [pltpu.VMEM((k_dev, e_dev, rows, cols), jnp.bfloat16)] * pieces,
             [pltpu.VMEM((k_dev, e_dev, rows, cols), jnp.bfloat16)] * (0 if two else pieces),
+            [turned] * pieces,
+            [turned] * (0 if two else pieces),
+            [turned] * (pieces if two else 0),
+            turned,
             pltpu.VMEM((chunks, 2, rows // 2, cols), jnp.bfloat16),
             pltpu.VMEM((chunks, 2, rows // 2, cols), jnp.bfloat16),
             pltpu.VMEM((chunks, 2, rows, cols), jnp.bfloat16),
+            dma((5,)),
         ]
         + [dma((pieces,))] * 8
         + [dma((chunks,))] * 6,
         compiler_params=pltpu.CompilerParams(
-            collective_id=0, has_side_effects=True, vmem_limit_bytes=48 * 2**20
+            collective_id=0, has_side_effects=True, vmem_limit_bytes=(59 if two else 60) * 2**20
         ),
         cost_estimate=pl.CostEstimate(flops=13 * 10**9, bytes_accessed=8 * 2**20, transcendentals=0),
-    )(phonon_pick, momentum_offsets, energy_map, green_blocks, hopping, phonons)
+    )(
+        phonon_pick, momentum_offsets.T, energy_map.T, green_blocks, hopping.reshape(-1, cols), phonons
+    )
 
 
 def solution(mesh):

time: 84.6 us -> 66.1 us (0.78)
  Pallas kernels: 73.5 us -> 61.4 us
  local copies, waits for them, and re-layouts: 10.8 us -> 4.6 us
    pallas_call x1, Pallas kernels: 73.5 us -> 61.4 us  [on_device(): pl.pallas_call(functools.partial(kernel, lax.axis_size('mom'), lax.axis_s...]
    unnamed x11 -> x1, local copies, waits for them, and re-layouts: 10.8 us -> 4.6 us
where the time goes in v1:
time: 66.1 us; the launch traced here: 66 us
  Pallas kernels  61.4 us (93%)
  local copies, waits for them, and re-layouts  4.6 us (7%)
    pallas_call x1, Pallas kernels, on_device(): pl.pallas_call(functools.partial(kernel, lax.axis_size('mom'), lax.axis_s...  61.4 us
    unnamed x1, local copies, waits for them, and re-layouts  4.6 us

profile of v1, /device:TPU:0, one launch (start us, length us, event | category | flops | bytes accessed | tf_op | source)
XLA Modules:
  0.0 66.0 jit_solution(14999133860470563090)
XLA Ops:
  0.0 61.4 %shard_map.64 = f32[2,2,2,2,256,256]{5,4,3,2,1,0:T(8,128)} custom-call(s32[4]{0:T(128)} %pick_in.1, s32[2,4]{1,0:T(2,128)} %bitcast.4, s32[2,4]{1,0:T(2,128)} %bitcast.5, bf16[2,2,2,2,256,256]{5,4,3,2,1,0:T(8,128)(2,1)} %green.1, bf16[768,256]{1,0:T(8,128)(2,1)} %bitcast.3, bf16[2,3,2,256,256]{4,3,2,1,0:T(8,128)(2,1)} %phon_in.1), custom_call_target="tpu_custom_call" | custom-call | flops 12999999488 | bytes 8388608 | tf_op jit(solution)/shard_map/pallas_call | solution.py:280
  61.4 4.6 %copy.8 = f32[2,2,2,2,256,256]{5,4,3,2,1,0:T(8,128)} copy(f32[2,2,2,2,256,256]{5,4,3,2,1,0:T(8,128)} %shard_map.64) | data formatting | bytes 8388608

commit v2 on v1

--- a/solution.py
+++ b/solution.py
@@ -230,8 +230,8 @@
         base + 7: [(far_turn, 2), (third, 1)],
         base + 8: [(third, 2)],
         base + 9: [
-            (sibling_far, 2), (arrived, 3), (fourth, 0), (fourth, 1), (fourth, 2),
-            (forward, 3), (far_turn, 3), (third, 3), (fourth, 3), (sibling_far, 3),
+            (forward, 3), (far_turn, 3), (third, 3), (sibling_far, 2), (sibling_far, 3),
+            (arrived, 3), (fourth, 0), (fourth, 1), (fourth, 2), (fourth, 3),
         ],
     }
     if two:
@@ -266,6 +266,39 @@
     lax.fori_loop(0, chunks, settle, 0)
 
 
+def settled(total):
+    rows = total.size // total.shape[-1]
+    flat = total.reshape(rows, total.shape[-1])
+
+    def move(src, dst, held, arrive, leave):
+        size = held.shape[1]
+        count = held.shape[0]
+        bring = [pltpu.make_async_copy(src.at[pl.ds(i * size, size)], held.at[i], arrive.at[i]) for i in range(count)]
+        take = [pltpu.make_async_copy(held.at[i], dst.at[pl.ds(i * size, size)], leave.at[i]) for i in range(count)]
+        for i in range(count):
+            bring[i].start()
+        for i in range(count):
+            bring[i].wait()
+            take[i].start()
+        for i in range(count):
+            take[i].wait()
+
+    parts = 8
+    return pl.pallas_call(
+        move,
+        out_shape=jax.ShapeDtypeStruct(flat.shape, flat.dtype),
+        in_specs=[pl.BlockSpec(memory_space=pl.ANY)],
+        out_specs=pl.BlockSpec(memory_space=pl.ANY),
+        scratch_shapes=[
+            pltpu.VMEM((parts, rows // parts, flat.shape[1]), flat.dtype),
+            pltpu.SemaphoreType.DMA((parts,)),
+            pltpu.SemaphoreType.DMA((parts,)),
+        ],
+        compiler_params=pltpu.CompilerParams(vmem_limit_bytes=60 * 2**20),
+        cost_estimate=pl.CostEstimate(flops=0, bytes_accessed=8 * 2**20, transcendentals=0),
+    )(flat).reshape(total.shape)
+
+
 def on_device(green_blocks, hopping, phonons, phonon_pick, momentum_offsets, energy_map):
     modes = hopping.shape[0]
     rows, cols = hopping.shape[1:]
@@ -277,7 +310,7 @@
     vmem = pl.BlockSpec(memory_space=pltpu.VMEM)
     hbm = pl.BlockSpec(memory_space=pl.ANY)
     turned = pltpu.VMEM((modes, k_dev, e_dev, rows, cols), jnp.float32)
-    return pl.pallas_call(
+    total = pl.pallas_call(
         functools.partial(kernel, lax.axis_size("mom"), lax.axis_size("en")),
         out_shape=jax.ShapeDtypeStruct(green_blocks.shape, jnp.float32),
         in_specs=[hbm] * 6,
@@ -309,6 +342,7 @@
     )(
         phonon_pick, momentum_offsets.T, energy_map.T, green_blocks, hopping.reshape(-1, cols), phonons
     )
+    return settled(total)
 
 
 def solution(mesh):

time: 66.1 us -> 65.1 us (0.985)
  local copies, waits for them, and re-layouts: 4.6 us -> 0 us
  Pallas kernels: 61.4 us -> 64.9 us
    unnamed x1 -> x0, local copies, waits for them, and re-layouts: 4.6 us -> none
    pallas_call x0 -> x1, Pallas kernels: none -> 3.58 us  [settled(): pl.pallas_call(move, out_shape=jax.ShapeDtypeStruct(flat.shape, flat.dtyp...]
where the time goes in v2:
time: 65.1 us; the launch traced here: 65 us
  Pallas kernels  64.9 us (100%)
    pallas_call x1, Pallas kernels, on_device(): pl.pallas_call(functools.partial(kernel, lax.axis_size('mom'), lax.axis_s...  61.4 us
    pallas_call x1, Pallas kernels, settled(): pl.pallas_call(move, out_shape=jax.ShapeDtypeStruct(flat.shape, flat.dtyp...  3.58 us

profile of v2, /device:TPU:0, one launch (start us, length us, event | category | flops | bytes accessed | tf_op | source)
XLA Modules:
  0.0 65.0 jit_solution(75303383403394645)
XLA Ops:
  0.0 61.4 %shard_map.64 = f32[2,2,2,2,256,256]{5,4,3,2,1,0:T(8,128)} custom-call(s32[4]{0:T(128)} %pick_in.1, s32[2,4]{1,0:T(2,128)} %bitcast.7, s32[2,4]{1,0:T(2,128)} %bitcast.8, bf16[2,2,2,2,256,256]{5,4,3,2,1,0:T(8,128)(2,1)} %green.1, bf16[768,256]{1,0:T(8,128)(2,1)} %bitcast.6, bf16[2,3,2,256,256]{4,3,2,1,0:T(8,128)(2,1)} %phon_in.1), custom_call_target="tpu_custom_call" | custom-call | flops 12999999488 | bytes 8388608 | tf_op jit(solution)/shard_map/pallas_call | solution.py:313
  61.4 3.6 %shard_map.65 = f32[4096,256]{1,0:T(8,128)} custom-call(f32[4096,256]{1,0:T(8,128)} %bitcast.5), custom_call_target="tpu_custom_call" | custom-call | bytes 8388608 | tf_op jit(solution)/shard_map/pallas_call | solution.py:287
